TPU v7x, 128 devices: a whole 4x4x4 slice. The times are simulated.
128 devices in a mesh: row: 8 (over z, core), col: 16 (over x, y).
Axes of the slice: x: 4, y: 4, z: 4, core: 2. Of those that a mesh axis runs over, the one named last changes fastest.
Arguments:
- front_panel: float32 [40960, 512], P('row', 'col'), may hold values from -16 to 48, as said below
- front_slab: float32 [40960, 8192], P('row', 'col'), may hold values from -6 to 6
- child_one: bfloat16 [8192, 8192], P('col', 'row'), may hold values from -6 to 6
- child_two: bfloat16 [8192, 8192], P('col', 'row'), may hold values from -6 to 6
- map_one: int32 [32], replicated, may hold values from 0 to 159, as said below
- map_two: int32 [32], replicated, may hold values from 0 to 159, as said below
Outputs:
- factor_panel: float32 [40960, 512], P('row', 'col')
- slab_out: float32 [40960, 8192], P('row', 'col')
Inputs may be any that keep to these rules, and one draw needn't show every extreme that they name: `front_panel`: its first 512 rows are, in all 512 columns, a symmetric positive definite block. `map_one`: distinct root row blocks. Of the 20 blocks of one index of row (numbers k * 20 to (k + 1) * 20 - 1) at most 8 are named, and exactly 8 for some index of row. `map_two`: as map_one, drawn independently.
All inputs are finite; a program needn't handle non-finite values.
Results may differ from a plain program's by a relative error of at most 0.0003.
Values may be sent and summed in bfloat16 or wider, within the bound.
A program may use at most 192 MiB of HBM per device.

v0:
```python
import jax
import jax.numpy as jnp
from jax import lax
from jax.sharding import PartitionSpec as P

P_SIZE = 256
BLK = 256


def from_root(value, axis, source):
    kept = jnp.where(lax.axis_index(axis) == source, value, 0).astype(value.dtype)
    return lax.psum(kept, axis)


def inverse_factor(block):
    lower = jnp.linalg.cholesky(block)
    identity = jnp.eye(P_SIZE, dtype=jnp.float32)
    return jax.scipy.linalg.solve_triangular(lower, identity, lower=True)


def diagonal_work(top):
    highest = lax.Precision.HIGHEST
    inverse_one = inverse_factor(top[:P_SIZE, :P_SIZE])
    first_top = jnp.dot(
        top[P_SIZE:, :P_SIZE], inverse_one.T, precision=highest, preferred_element_type=jnp.float32
    )
    second_top = top[P_SIZE:, P_SIZE:] - jnp.dot(
        first_top, first_top.T, precision=highest, preferred_element_type=jnp.float32
    )
    inverse_two = inverse_factor(second_top)
    return (inverse_one, first_top, inverse_two)


def panel_rows(panel, inverse_one, first_top, inverse_two):
    highest = lax.Precision.HIGHEST
    first_cols = jnp.dot(
        panel[:, :P_SIZE], inverse_one.T, precision=highest, preferred_element_type=jnp.float32
    )
    second_in = panel[:, P_SIZE:] - jnp.dot(
        first_cols, first_top.T, precision=highest, preferred_element_type=jnp.float32
    )
    second_cols = jnp.dot(
        second_in, inverse_two.T, precision=highest, preferred_element_type=jnp.float32
    )
    return jnp.concatenate([first_cols, second_cols], 1)


def routing(mapping, local_blocks, row_count):
    owner = mapping // local_blocks
    owner_hot = (owner[:, None] == jnp.arange(row_count, dtype=jnp.int32)[None, :]).astype(
        jnp.int32
    )
    rank = jnp.sum(owner_hot * (jnp.cumsum(owner_hot, 0) - 1), 1)
    return (owner, rank, mapping % local_blocks)


def per_device(front_panel, front_slab, child_one, child_two, map_one, map_two):
    rows_dev = front_slab.shape[0]
    slab_width = front_slab.shape[1]
    panel_width = front_panel.shape[1]
    child_blocks = map_one.shape[0]
    child_local = child_one.shape[0]
    row_count = lax.axis_size("row")
    col_count = lax.axis_size("col")
    row_rank = lax.axis_index("row")
    col_rank = lax.axis_index("col")
    piece = slab_width // row_count
    local_blocks = rows_dev // BLK
    capacity = 2 * child_blocks // row_count

    def split_columns(child):
        return child.reshape(child_local, col_count, piece)

    got_one, got_two = (
        lax.all_to_all(split_columns(child_one), "col", split_axis=1, concat_axis=0, tiled=True),
        lax.all_to_all(split_columns(child_two), "col", split_axis=1, concat_axis=0, tiled=True),
    )

    def send_rows(received, mapping):
        owner, rank, target = routing(mapping, local_blocks, row_count)
        slot = owner * capacity + rank
        select = (
            slot[None, :] == jnp.arange(row_count * capacity, dtype=jnp.int32)[:, None]
        ).astype(jnp.bfloat16)
        blocks = received.reshape(child_blocks, BLK * piece)
        packed = jnp.dot(select, blocks, preferred_element_type=jnp.float32).astype(jnp.bfloat16)
        return packed.reshape(row_count * capacity * BLK, piece)

    arrived_one, arrived_two = (
        lax.all_to_all(send_rows(got_one, map_one), "row", split_axis=0, concat_axis=1, tiled=True),
        lax.all_to_all(send_rows(got_two, map_two), "row", split_axis=0, concat_axis=1, tiled=True),
    )

    def place(arrived, mapping):
        owner, rank, target = routing(mapping, local_blocks, row_count)
        mine = (owner == row_rank)[None, :, None]
        at_block = target[None, :, None] == jnp.arange(local_blocks, dtype=jnp.int32)[:, None, None]
        at_slot = rank[None, :, None] == jnp.arange(capacity, dtype=jnp.int32)[None, None, :]
        placing = jnp.sum((at_block & at_slot & mine).astype(jnp.int32), 1).astype(jnp.bfloat16)
        added = jnp.dot(
            placing, arrived.reshape(capacity, BLK * slab_width), preferred_element_type=jnp.float32
        )
        return added.reshape(rows_dev, slab_width)

    assembled = front_slab + place(arrived_one, map_one) + place(arrived_two, map_two)
    gathered = lax.all_gather(front_panel, "col", axis=1, tiled=True)
    top = gathered[: 2 * P_SIZE]
    top = from_root(top, "row", 0)
    inverse_one, first_top, inverse_two = diagonal_work(top)
    factor = panel_rows(gathered, inverse_one, first_top, inverse_two)
    factor_out = lax.dynamic_slice_in_dim(factor, col_rank * panel_width, panel_width, 1)
    global_rows = row_rank * rows_dev + jnp.arange(rows_dev, dtype=jnp.int32)
    masked = factor * (global_rows >= 2 * P_SIZE)[:, None].astype(jnp.float32)
    wanted = (
        2 * P_SIZE
        + col_rank * slab_width
        + jnp.arange(slab_width, dtype=jnp.int32)
        - row_rank * rows_dev
    )
    valid = ((wanted >= 0) & (wanted < rows_dev))[:, None].astype(jnp.float32)
    picked = jnp.take(factor, jnp.clip(wanted, 0, rows_dev - 1), axis=0) * valid
    slab_rows = lax.psum(picked, "row")
    update = jnp.dot(
        masked, slab_rows.T, precision=lax.Precision.HIGHEST, preferred_element_type=jnp.float32
    )
    return (factor_out, assembled - update)


def solution(mesh):
    in_specs = (P("row", "col"), P("row", "col"), P("col", "row"), P("col", "row"), P(), P())
    out_specs = (P("row", "col"), P("row", "col"))
    return jax.shard_map(
        per_device, mesh=mesh, in_specs=in_specs, out_specs=out_specs, check_vma=False
    )
```

profile of v0, /device:TPU:0, one launch (start us, length us, event | category | flops | bytes accessed | tf_op | source)
XLA Modules:
  0.0 495.1 jit_solution(5786572889173300262)
XLA Ops:
  10.2 7.1 %all-to-all-start = ((bf16[512,16,64]{0,2,1:T(8,128)(2,1)}), bf16[512,16,64]{0,2,1:T(8,128)(2,1)S(1)}, u32[]{:S(2)}, u32[]{:S(2)}) async-start(bf16[512,16,64]{0,2,1:T(8,128)(2,1)} %bitcast.11), calls=%async_computation | async-start | bytes 2097152 | tf_op jit(solution)/shard_map/all_to_all | solution.py:75
  18.7 19.1 %all-to-all-done = bf16[512,16,64]{0,2,1:T(8,128)(2,1)S(1)} async-done(((bf16[512,16,64]{0,2,1:T(8,128)(2,1)}), bf16[512,16,64]{0,2,1:T(8,128)(2,1)S(1)}, u32[]{:S(2)}, u32[]{:S(2)}) %all-to-all-start) | async-done | bytes 1048608 | tf_op jit(solution)/shard_map/all_to_all | solution.py:75
  37.8 6.6 %all-to-all-start.2 = ((bf16[512,16,64]{0,2,1:T(8,128)(2,1)}), bf16[512,16,64]{0,2,1:T(8,128)(2,1)S(1)}, u32[]{:S(2)}, u32[]{:S(2)}) async-start(bf16[512,16,64]{0,2,1:T(8,128)(2,1)} %bitcast.15), calls=%async_computation.2 | async-start | bytes 2097152 | tf_op jit(solution)/shard_map/all_to_all | solution.py:76
  51.2 5.5 %all_to_all.49 = bf16[8,2048,64]{2,1,0:T(8,128)(2,1)} reshape(bf16[64,16384]{1,0:T(8,128)(2,1)S(1)} %convolution_convert_fusion.1) | data formatting | bytes 4194304 | tf_op jit(solution)/shard_map/all_to_all | solution.py:90
  56.7 4.8 copy.41
  61.5 6.5 %all-to-all-start.1 = ((bf16[8,2048,64]{1,2,0:T(8,128)(2,1)}), bf16[8,2048,64]{1,2,0:T(8,128)(2,1)S(1)}, u32[]{:S(2)}, u32[]{:S(2)}) async-start(bf16[8,2048,64]{1,2,0:T(8,128)(2,1)} %copy.41), calls=%async_computation.1 | async-start | bytes 4194304 | tf_op jit(solution)/shard_map/all_to_all | solution.py:90
  75.1 6.5 %all_to_all.55 = bf16[8,2048,64]{2,1,0:T(8,128)(2,1)} reshape(bf16[64,16384]{1,0:T(8,128)(2,1)} %convolution_convert_fusion) | data formatting | bytes 4194304 | tf_op jit(solution)/shard_map/all_to_all | solution.py:91
  86.4 8.9 %all-to-all-done.1 = bf16[8,2048,64]{1,2,0:T(8,128)(2,1)S(1)} async-done(((bf16[8,2048,64]{1,2,0:T(8,128)(2,1)}), bf16[8,2048,64]{1,2,0:T(8,128)(2,1)S(1)}, u32[]{:S(2)}, u32[]{:S(2)}) %all-to-all-start.1) | async-done | bytes 2097184 | tf_op jit(solution)/shard_map/all_to_all | solution.py:90
  105.0 5.0 %reshape.232 = bf16[1048576]{0:T(1024)(128)(2,1)S(1)} reshape(bf16[2048,8,64]{2,1,0:T(8,128)(2,1)} %copy.42) | data formatting | bytes 4194304
  112.3 7.9 %fusion.38 = f32[20,131072]{1,0:T(8,128)} fusion(bf16[8,131072]{1,0:T(8,128)(2,1)} %reshape.194, s32[20,8]{1,0:T(8,128)S(1)} %convert_reduce_fusion.1), kind=kOutput, calls=%fused_computation.86 | convolution fusion | flops 41943200 | bytes 12583552 | tf_op jit(solution)/shard_map/dot_general | solution.py:100
  120.2 10.5 %reshape.195 = f32[5120,512]{1,0:T(8,128)} reshape(f32[20,131072]{1,0:T(8,128)} %fusion.38) | data formatting | bytes 20971520 | tf_op jit(solution)/shard_map/reshape | solution.py:103
  130.7 5.6 %copy.46 = bf16[2048,8,64]{2,1,0:T(8,128)(2,1)} copy(bf16[2048,8,64]{0,2,1:T(8,128)(2,1)} %bitcast.18) | data formatting | bytes 4194304 | tf_op jit(solution)/shard_map/all_to_all | solution.py:91
  136.4 5.0 %reshape.230 = bf16[1048576]{0:T(1024)(128)(2,1)S(1)} reshape(bf16[2048,8,64]{2,1,0:T(8,128)(2,1)} %copy.46) | data formatting | bytes 4194304
  146.0 7.9 %fusion.36 = f32[20,131072]{1,0:T(8,128)} fusion(bf16[8,131072]{1,0:T(8,128)(2,1)} %reshape.198, s32[20,8]{1,0:T(8,128)S(1)} %convert_reduce_fusion), kind=kOutput, calls=%fused_computation.84 | convolution fusion | flops 41943200 | bytes 12583552 | tf_op jit(solution)/shard_map/dot_general | solution.py:100
  153.9 11.0 %reshape.199 = f32[5120,512]{1,0:T(8,128)} reshape(f32[20,131072]{1,0:T(8,128)} %fusion.36) | data formatting | bytes 20971520 | tf_op jit(solution)/shard_map/reshape | solution.py:103
  164.9 45.9 %all-reduce.4.cloned.1.call-done = f32[512,512]{0,1:T(8,128)} async-done(((f32[512,512]{0,1:T(8,128)}), f32[512,512]{0,1:T(8,128)}) %all-reduce.4.cloned.1.call-update) | async-done | bytes 1048592 | tf_op jit(solution)/shard_map/psum | solution.py:12
  213.1 11.7 %cholesky.130 = f32[128,128]{1,0:T(8,128)S(1)} custom-call(f32[128,128]{1,0:T(8,128)S(1)} %cholesky.194), custom_call_target="Cholesky" | custom-call | tf_op jit(solution)/shard_map/jit(cholesky)/cholesky | solution.py:16
  224.8 9.8 %custom-call.13 = f32[1,128,128]{1,2,0:T(8,128)S(1)} custom-call(f32[1,128,128]{2,1,0:T(8,128)S(1)} %get-tuple-element.51), custom_call_target="InvertDiagBlocksLowerTriangular" | custom-call | tf_op jit(solution)/shard_map/jit(cholesky)/cholesky | solution.py:16
  235.1 11.7 %cholesky.147 = f32[128,128]{1,0:T(8,128)S(1)} custom-call(f32[128,128]{1,0:T(8,128)S(1)} %convolution_subtract_fusion.5), custom_call_target="Cholesky" | custom-call | tf_op jit(solution)/shard_map/jit(cholesky)/cholesky | solution.py:16
  252.8 19.8 %custom-call.14 = f32[2,128,128]{1,2,0:T(8,128)S(1)} custom-call(f32[2,128,128]{2,1,0:T(8,128)S(1)} %get-tuple-element.18), custom_call_target="InvertDiagBlocksLowerTriangular" | custom-call | tf_op jit(solution)/shard_map/jit(_solve_triangular)/triangular_solve | solution.py:18
  274.8 11.7 %cholesky.164 = f32[128,128]{1,0:T(8,128)S(1)} custom-call(f32[128,128]{1,0:T(8,128)S(1)} %cholesky.197), custom_call_target="Cholesky" | custom-call | tf_op jit(solution)/shard_map/jit(cholesky)/cholesky | solution.py:16
  286.5 9.8 %custom-call.15 = f32[1,128,128]{1,2,0:T(8,128)S(1)} custom-call(f32[1,128,128]{2,1,0:T(8,128)S(1)} %get-tuple-element.47), custom_call_target="InvertDiagBlocksLowerTriangular" | custom-call | tf_op jit(solution)/shard_map/jit(cholesky)/cholesky | solution.py:16
  296.8 11.7 %cholesky.181 = f32[128,128]{1,0:T(8,128)S(1)} custom-call(f32[128,128]{1,0:T(8,128)S(1)} %convolution_subtract_fusion.4), custom_call_target="Cholesky" | custom-call | tf_op jit(solution)/shard_map/jit(cholesky)/cholesky | solution.py:16
  315.4 19.9 %custom-call.16 = f32[2,128,128]{1,2,0:T(8,128)S(1)} custom-call(f32[2,128,128]{2,1,0:T(8,128)S(1)} %get-tuple-element.19), custom_call_target="InvertDiagBlocksLowerTriangular" | custom-call | tf_op jit(solution)/shard_map/jit(_solve_triangular)/triangular_solve | solution.py:18
  336.2 6.7 %fusion.4 = f32[256,5120]{1,0:T(8,128)S(1)} fusion(f32[5120,512]{0,1:T(8,128)} %all-gather.2.cloned.1.call-done, f32[128,256]{1,0:T(8,128)S(1)} %fusion.26, f32[128,256]{1,0:T(8,128)S(1)} %fusion.19), kind=kOutput, calls=%fused_computation.14 | convolution fusion | flops 4026597376 | bytes 10747904 | tf_op jit(solution)/shard_map/dot_general | solution.py:36
  342.9 9.0 %convolution_subtract_fusion = f32[5120,256]{0,1:T(8,128)S(1)} fusion(f32[256,5120]{1,0:T(8,128)S(1)} %fusion.4, f32[256,256]{1,0:T(8,128)S(1)} %fusion.8, f32[5120,512]{0,1:T(8,128)} %all-gather.2.cloned.1.call-done), kind=kOutput, calls=%fused_computation.13 | convolution fusion | flops 4027842560 | bytes 15990784 | tf_op jit(solution)/shard_map/dot_general | solution.py:39
  351.9 6.5 %fusion.10 = f32[5120,256]{0,1:T(8,128)} fusion(f32[5120,256]{0,1:T(8,128)S(1)} %convolution_subtract_fusion, f32[128,256]{1,0:T(8,128)S(1)} %fusion.22, f32[128,256]{1,0:T(8,128)S(1)} %fusion.17), kind=kOutput, calls=%fused_computation.30 | convolution fusion | flops 4026597376 | bytes 10747904 | tf_op jit(solution)/shard_map/dot_general | solution.py:42
  358.4 9.3 %pad_maximum_fusion = f32[5120,512]{0,1:T(8,128)} fusion(f32[5120,256]{0,1:T(8,128)} %fusion.10, f32[5120,256]{0,1:T(8,128)} %bitcast.92), kind=kLoop, calls=%fused_computation.8 | loop fusion | flops 2621440 | bytes 20971520 | tf_op jit(solution)/shard_map/concatenate | solution.py:45
  367.7 11.4 %copy.47 = f32[5120,512]{1,0:T(8,128)} copy(f32[5120,512]{0,1:T(8,128)} %pad_maximum_fusion) | data formatting | bytes 20971520 | tf_op jit(solution)/shard_map/concatenate | solution.py:45
  379.1 6.2 %gather_fusion = f32[512,512]{1,0:T(8,128)S(1)} fusion(f32[5120,512]{1,0:T(8,128)} %copy.47, s32[1024]{0:T(1024)S(1)} %pad_clamp_fusion), kind=kCustom, calls=%fused_computation | custom fusion | bytes 2099200 | tf_op jit(solution)/shard_map/jit(_take)/gather | solution.py:121
  388.6 60.0 %all-reduce.6.cloned.1.call-done = f32[512,512]{1,0:T(8,128)} async-done(((f32[512,512]{1,0:T(8,128)}), f32[512,512]{1,0:T(8,128)}) %all-reduce.6.cloned.1.call-update) | async-done | bytes 1048592 | tf_op jit(solution)/shard_map/psum | solution.py:122
  448.6 39.6 %add_subtract_fusion = f32[5120,512]{1,0:T(8,128)} fusion(f32[5120,512]{1,0:T(8,128)} %reshape.199, f32[5120,512]{1,0:T(8,128)} %param.10, f32[5120,512]{1,0:T(8,128)} %reshape.195, f32[512,512]{1,0:T(8,128)} %all-reduce.6.cloned.1.call-done, f32[5120]{0:T(1024)S(1)} %fusion.31, f32[5120,256]{0,1:T(8,128)} %fusion.10, f32[5120,256]{0,1:T(8,128)} %bitcast.94), kind=kOutput, calls=%fused_computation.12 | convolution fusion | flops 16119234560 | bytes 53497856 | tf_op jit(solution)/shard_map/dot_general | solution.py:123
  (106 shorter events, 66.8 us)
Async XLA Ops:
  7.2 10.2 %copy-start.3 = (bf16[512,1024]{1,0:T(8,128)(2,1)S(1)}, bf16[512,1024]{1,0:T(8,128)(2,1)}, u32[]{:S(2)}) copy-start(bf16[512,1024]{1,0:T(8,128)(2,1)} %param.12) | copy-start | bytes 3145732
  7.2 37.2 %copy-start.5 = (s32[32]{0:T(128)S(1)}, s32[32]{0:T(128)}, u32[]{:S(2)}) copy-start(s32[32]{0:T(128)} %param.13) | copy-start | bytes 388
  7.2 37.2 %copy-start.4 = (s32[32]{0:T(128)S(1)}, s32[32]{0:T(128)}, u32[]{:S(2)}) copy-start(s32[32]{0:T(128)} %param.14) | copy-start | bytes 388
  7.2 136.4 %all-gather.2.cloned.1.call-start = ((), (), s32[]{:S(2)}) async-start(), calls=%async_computation.4 | async-start | bytes 11141120 | tf_op jit(solution)/shard_map/all_gather | solution.py:106
  10.2 27.6 %all-to-all-start = ((bf16[512,16,64]{0,2,1:T(8,128)(2,1)}), bf16[512,16,64]{0,2,1:T(8,128)(2,1)S(1)}, u32[]{:S(2)}, u32[]{:S(2)}) async-start(bf16[512,16,64]{0,2,1:T(8,128)(2,1)} %bitcast.11), calls=%async_computation | async-start | bytes 2097152 | tf_op jit(solution)/shard_map/all_to_all | solution.py:75
  37.8 7.0 %copy-start.1 = (bf16[512,16,64]{0,2,1:T(8,128)(2,1)}, bf16[512,16,64]{0,2,1:T(8,128)(2,1)S(1)}, u32[]{:S(2)}) copy-start(bf16[512,16,64]{0,2,1:T(8,128)(2,1)S(1)} %all-to-all-done) | copy-start | bytes 3145732
  37.8 23.7 %all-to-all-start.2 = ((bf16[512,16,64]{0,2,1:T(8,128)(2,1)}), bf16[512,16,64]{0,2,1:T(8,128)(2,1)S(1)}, u32[]{:S(2)}, u32[]{:S(2)}) async-start(bf16[512,16,64]{0,2,1:T(8,128)(2,1)} %bitcast.15), calls=%async_computation.2 | async-start | bytes 2097152 | tf_op jit(solution)/shard_map/all_to_all | solution.py:76
  61.5 33.7 %all-to-all-start.1 = ((bf16[8,2048,64]{1,2,0:T(8,128)(2,1)}), bf16[8,2048,64]{1,2,0:T(8,128)(2,1)S(1)}, u32[]{:S(2)}, u32[]{:S(2)}) async-start(bf16[8,2048,64]{1,2,0:T(8,128)(2,1)} %copy.41), calls=%async_computation.1 | async-start | bytes 4194304 | tf_op jit(solution)/shard_map/all_to_all | solution.py:90
  95.2 35.5 %all-to-all-start.3 = ((bf16[8,2048,64]{1,2,0:T(8,128)(2,1)}), bf16[8,2048,64]{1,2,0:T(8,128)(2,1)}, u32[]{:S(2)}, u32[]{:S(2)}) async-start(bf16[8,2048,64]{1,2,0:T(8,128)(2,1)} %copy.45), calls=%async_computation.3 | async-start | bytes 4194304 | tf_op jit(solution)/shard_map/all_to_all | solution.py:91
  99.6 111.3 %all-reduce.4.cloned.1.call-start = ((), (), s32[]{:S(2)}) async-start(), calls=%async_computation.5 | async-start | bytes 2097152 | tf_op jit(solution)/shard_map/psum | solution.py:12
  146.0 302.6 %all-reduce.6.cloned.1.call-start = ((), (), s32[]{:S(2)}) async-start(), calls=%async_computation.6 | async-start | bytes 2097152 | tf_op jit(solution)/shard_map/psum | solution.py:122
  210.9 62.7 %copy-start.2 = (f32[512,512]{0,1:T(8,128)S(1)}, f32[512,512]{0,1:T(8,128)}, u32[]{:S(2)}) copy-start(f32[512,512]{0,1:T(8,128)} %all-reduce.4.cloned.1.call-done) | copy-start | bytes 3145732
  342.9 9.0 %copy-start = (f32[256,5120]{1,0:T(8,128)}, f32[256,5120]{1,0:T(8,128)S(1)}, u32[]{:S(2)}) copy-start(f32[256,5120]{1,0:T(8,128)S(1)} %fusion.4) | copy-start | bytes 15728644
Sparse Core Ops, SparseCore 0:
  10.2 89.2 all-gather.1
  146.1 64.7 all-reduce.3
  386.7 61.7 all-reduce.5
where the time goes:
time: 502 us; the launch traced here: 495 us
  waiting for transfers between devices  135 us (27%)
  other arithmetic  126 us (25%)
  local copies, waits for them, and re-layouts  107 us (21%)
  matrix products  85.3 us (17%)
  starting transfers between devices  24.9 us (5%)
  between operations  17.2 us (3%)
    another operation x13, other arithmetic, inverse_factor(): lower = jnp.linalg.cholesky(block)  68.6 us
    psum x1, waiting for transfers between devices, per_device(): slab_rows = lax.psum(picked, 'row')  60 us
    psum x1, waiting for transfers between devices, from_root(): return lax.psum(kept, axis)  45.9 us
    another operation x5, other arithmetic, inverse_factor(): return jax.scipy.linalg.solve_triangular(lower, identity, lower=True)  39.8 us
    dot_general x1, matrix products, per_device(): jnp.dot(masked, slab_rows.T, precision=lax.Precision.HIGHEST, preferred_e...  39.6 us
    reshape x2, local copies, waits for them, and re-layouts, place(): return added.reshape(rows_dev, slab_width)  21.5 us
    all_to_all x1, waiting for transfers between devices, per_device(): lax.all_to_all(split_columns(child_one), 'col', split_axis=1, concat_axis...  19.1 us
    all_to_all x3, local copies, waits for them, and re-layouts, per_device(): lax.all_to_all(send_rows(got_two, map_two), 'row', split_axis=0, concat_a...  16.9 us
  transfers between devices with their start and end apart: 7, of which 4 were waited for; matrix products, arithmetic and copies ran while one was open for 18% of the time, Pallas kernels for 0%

commit v1 on v0

--- a/solution.py
+++ b/solution.py
@@ -71,8 +71,19 @@
     def split_columns(child):
         return child.reshape(child_local, col_count, piece)
 
+    def deliver_modes(work_x, pos_dim, join_dim):
+        return jnp.concatenate(
+            jax.lax.all_to_all(
+                jnp.stack(jnp.split(work_x, jax.lax.psum(1, axis_name="col"), pos_dim)),
+                axis_name="col",
+                split_axis=0,
+                concat_axis=0,
+            ),
+            join_dim,
+        )
+
     got_one, got_two = (
-        lax.all_to_all(split_columns(child_one), "col", split_axis=1, concat_axis=0, tiled=True),
+        deliver_modes(split_columns(child_one), 1, 0),
         lax.all_to_all(split_columns(child_two), "col", split_axis=1, concat_axis=0, tiled=True),
     )
 

time: 502 us -> 518 us (1.032)
  local copies, waits for them, and re-layouts: 107 us -> 117 us
  waiting for transfers between devices: 135 us -> 145 us
    unnamed x16 -> x31, local copies, waits for them, and re-layouts: 13.7 us -> 22.5 us
    all_to_all x1, waiting for transfers between devices: 0.01 us -> 7.01 us  [per_device(): lax.all_to_all(split_columns(child_two), 'col', split_axis=1, concat_axis...]
  transfers between devices with their start and end apart: 7 -> 7, of which waited for: 4 -> 5; matrix products, arithmetic and copies ran while one was open for 18% -> 20% of each run, Pallas kernels for 0% -> 0%
where the time goes in v1:
time: 518 us; the launch traced here: 510 us
  waiting for transfers between devices  145 us (28%)
  other arithmetic  126 us (24%)
  local copies, waits for them, and re-layouts  117 us (23%)
  matrix products  85.3 us (16%)
  starting transfers between devices  20.4 us (4%)
  between operations  17.2 us (3%)
    another operation x13, other arithmetic, inverse_factor(): lower = jnp.linalg.cholesky(block)  68.6 us
    psum x1, waiting for transfers between devices, per_device(): slab_rows = lax.psum(picked, 'row')  60 us
    psum x1, waiting for transfers between devices, from_root(): return lax.psum(kept, axis)  45.3 us
    another operation x5, other arithmetic, inverse_factor(): return jax.scipy.linalg.solve_triangular(lower, identity, lower=True)  39.8 us
    dot_general x1, matrix products, per_device(): jnp.dot(masked, slab_rows.T, precision=lax.Precision.HIGHEST, preferred_e...  39.6 us
    all_to_all x1, waiting for transfers between devices, deliver_modes(): jax.lax.all_to_all(jnp.stack(jnp.split(work_x, jax.lax.psum(1, axis_name=...  22.9 us
    unnamed x31, local copies, waits for them, and re-layouts  22.5 us
    reshape x2, local copies, waits for them, and re-layouts, place(): return added.reshape(rows_dev, slab_width)  21.6 us
  transfers between devices with their start and end apart: 7, of which 5 were waited for; matrix products, arithmetic and copies ran while one was open for 20% of the time, Pallas kernels for 0%

profile of v1, /device:TPU:0, one launch (start us, length us, event | category | flops | bytes accessed | tf_op | source)
XLA Modules:
  0.0 510.3 jit_solution(7957695563744607867)
XLA Ops:
  19.6 7.1 %all-to-all-start = ((bf16[16,512,1,64]{1,3,2,0:T(8,128)(2,1)}), bf16[16,512,1,64]{1,3,2,0:T(8,128)(2,1)S(1)}, u32[]{:S(2)}, u32[]{:S(2)}) async-start(bf16[16,512,1,64]{1,3,2,0:T(8,128)(2,1)} %fusion.21), calls=%async_computation | async-start | bytes 2097152 | tf_op jit(solution)/shard_map/all_to_all | solution.py:76
  28.1 22.9 %all-to-all-done = bf16[16,512,1,64]{1,3,2,0:T(8,128)(2,1)S(1)} async-done(((bf16[16,512,1,64]{1,3,2,0:T(8,128)(2,1)}), bf16[16,512,1,64]{1,3,2,0:T(8,128)(2,1)S(1)}, u32[]{:S(2)}, u32[]{:S(2)}) %all-to-all-start) | async-done | bytes 1048608 | tf_op jit(solution)/shard_map/all_to_all | solution.py:76
  61.5 5.5 %all_to_all.39 = bf16[8,2048,64]{2,1,0:T(8,128)(2,1)} reshape(bf16[64,16384]{1,0:T(8,128)(2,1)S(1)} %convolution_convert_fusion.1) | data formatting | bytes 4194304 | tf_op jit(solution)/shard_map/all_to_all | solution.py:101
  67.0 4.8 copy.56
  71.8 7.0 %all-to-all-done.2 = bf16[512,16,64]{0,2,1:T(8,128)(2,1)S(1)} async-done(((bf16[512,16,64]{0,2,1:T(8,128)(2,1)}), bf16[512,16,64]{0,2,1:T(8,128)(2,1)S(1)}, u32[]{:S(2)}, u32[]{:S(2)}) %all-to-all-start.2) | async-done | bytes 1048608 | tf_op jit(solution)/shard_map/all_to_all | solution.py:87
  78.8 5.0 all-to-all-start.1
  90.9 6.5 %all_to_all.45 = bf16[8,2048,64]{2,1,0:T(8,128)(2,1)} reshape(bf16[64,16384]{1,0:T(8,128)(2,1)} %convolution_convert_fusion) | data formatting | bytes 4194304 | tf_op jit(solution)/shard_map/all_to_all | solution.py:102
  102.1 8.9 %all-to-all-done.1 = bf16[8,2048,64]{1,2,0:T(8,128)(2,1)S(1)} async-done(((bf16[8,2048,64]{1,2,0:T(8,128)(2,1)}), bf16[8,2048,64]{1,2,0:T(8,128)(2,1)S(1)}, u32[]{:S(2)}, u32[]{:S(2)}) %all-to-all-start.1) | async-done | bytes 2097184 | tf_op jit(solution)/shard_map/all_to_all | solution.py:101
  120.8 5.0 reshape.227
  128.0 7.9 %fusion.54 = f32[20,131072]{1,0:T(8,128)} fusion(bf16[8,131072]{1,0:T(8,128)(2,1)} %reshape.189, s32[20,8]{1,0:T(8,128)S(1)} %convert_reduce_fusion.1), kind=kOutput, calls=%fused_computation.118 | convolution fusion | flops 41943200 | bytes 12583552 | tf_op jit(solution)/shard_map/dot_general | solution.py:111
  136.0 10.5 %reshape.190 = f32[5120,512]{1,0:T(8,128)} reshape(f32[20,131072]{1,0:T(8,128)} %fusion.54) | data formatting | bytes 20971520 | tf_op jit(solution)/shard_map/reshape | solution.py:114
  146.5 5.6 %copy.61 = bf16[2048,8,64]{2,1,0:T(8,128)(2,1)} copy(bf16[2048,8,64]{0,2,1:T(8,128)(2,1)} %bitcast.32) | data formatting | bytes 4194304 | tf_op jit(solution)/shard_map/all_to_all | solution.py:102
  152.1 5.0 reshape.225
  161.8 7.9 %fusion.52 = f32[20,131072]{1,0:T(8,128)} fusion(bf16[8,131072]{1,0:T(8,128)(2,1)} %reshape.193, s32[20,8]{1,0:T(8,128)S(1)} %convert_reduce_fusion), kind=kOutput, calls=%fused_computation.116 | convolution fusion | flops 41943200 | bytes 12583552 | tf_op jit(solution)/shard_map/dot_general | solution.py:111
  169.7 11.1 %reshape.194 = f32[5120,512]{1,0:T(8,128)} reshape(f32[20,131072]{1,0:T(8,128)} %fusion.52) | data formatting | bytes 20971520 | tf_op jit(solution)/shard_map/reshape | solution.py:114
  180.8 45.3 %all-reduce.4.cloned.1.call-done = f32[512,512]{0,1:T(8,128)} async-done(((f32[512,512]{0,1:T(8,128)}), f32[512,512]{0,1:T(8,128)}) %all-reduce.4.cloned.1.call-update) | async-done | bytes 1048592 | tf_op jit(solution)/shard_map/psum | solution.py:12
  228.2 11.7 %cholesky.130 = f32[128,128]{1,0:T(8,128)S(1)} custom-call(f32[128,128]{1,0:T(8,128)S(1)} %cholesky.194), custom_call_target="Cholesky" | custom-call | tf_op jit(solution)/shard_map/jit(cholesky)/cholesky | solution.py:16
  240.0 9.8 %custom-call.13 = f32[1,128,128]{1,2,0:T(8,128)S(1)} custom-call(f32[1,128,128]{2,1,0:T(8,128)S(1)} %get-tuple-element.51), custom_call_target="InvertDiagBlocksLowerTriangular" | custom-call | tf_op jit(solution)/shard_map/jit(cholesky)/cholesky | solution.py:16
  250.3 11.7 %cholesky.147 = f32[128,128]{1,0:T(8,128)S(1)} custom-call(f32[128,128]{1,0:T(8,128)S(1)} %convolution_subtract_fusion.5), custom_call_target="Cholesky" | custom-call | tf_op jit(solution)/shard_map/jit(cholesky)/cholesky | solution.py:16
  267.9 19.8 %custom-call.14 = f32[2,128,128]{1,2,0:T(8,128)S(1)} custom-call(f32[2,128,128]{2,1,0:T(8,128)S(1)} %get-tuple-element.18), custom_call_target="InvertDiagBlocksLowerTriangular" | custom-call | tf_op jit(solution)/shard_map/jit(_solve_triangular)/triangular_solve | solution.py:18
  289.9 11.7 %cholesky.164 = f32[128,128]{1,0:T(8,128)S(1)} custom-call(f32[128,128]{1,0:T(8,128)S(1)} %cholesky.197), custom_call_target="Cholesky" | custom-call | tf_op jit(solution)/shard_map/jit(cholesky)/cholesky | solution.py:16
  301.7 9.8 %custom-call.15 = f32[1,128,128]{1,2,0:T(8,128)S(1)} custom-call(f32[1,128,128]{2,1,0:T(8,128)S(1)} %get-tuple-element.47), custom_call_target="InvertDiagBlocksLowerTriangular" | custom-call | tf_op jit(solution)/shard_map/jit(cholesky)/cholesky | solution.py:16
  312.0 11.7 %cholesky.181 = f32[128,128]{1,0:T(8,128)S(1)} custom-call(f32[128,128]{1,0:T(8,128)S(1)} %convolution_subtract_fusion.4), custom_call_target="Cholesky" | custom-call | tf_op jit(solution)/shard_map/jit(cholesky)/cholesky | solution.py:16
  330.5 19.9 %custom-call.16 = f32[2,128,128]{1,2,0:T(8,128)S(1)} custom-call(f32[2,128,128]{2,1,0:T(8,128)S(1)} %get-tuple-element.19), custom_call_target="InvertDiagBlocksLowerTriangular" | custom-call | tf_op jit(solution)/shard_map/jit(_solve_triangular)/triangular_solve | solution.py:18
  351.3 6.7 %fusion.4 = f32[256,5120]{1,0:T(8,128)S(1)} fusion(f32[5120,512]{0,1:T(8,128)} %all-gather.2.cloned.1.call-done, f32[128,256]{1,0:T(8,128)S(1)} %fusion.42, f32[128,256]{1,0:T(8,128)S(1)} %fusion.19), kind=kOutput, calls=%fused_computation.14 | convolution fusion | flops 4026597376 | bytes 10747904 | tf_op jit(solution)/shard_map/dot_general | solution.py:36
  358.0 9.0 %convolution_subtract_fusion = f32[5120,256]{0,1:T(8,128)S(1)} fusion(f32[256,5120]{1,0:T(8,128)S(1)} %fusion.4, f32[256,256]{1,0:T(8,128)S(1)} %fusion.8, f32[5120,512]{0,1:T(8,128)} %all-gather.2.cloned.1.call-done), kind=kOutput, calls=%fused_computation.13 | convolution fusion | flops 4027842560 | bytes 15990784 | tf_op jit(solution)/shard_map/dot_general | solution.py:39
  367.0 6.5 %fusion.10 = f32[5120,256]{0,1:T(8,128)} fusion(f32[5120,256]{0,1:T(8,128)S(1)} %convolution_subtract_fusion, f32[128,256]{1,0:T(8,128)S(1)} %fusion.38, f32[128,256]{1,0:T(8,128)S(1)} %fusion.17), kind=kOutput, calls=%fused_computation.30 | convolution fusion | flops 4026597376 | bytes 10747904 | tf_op jit(solution)/shard_map/dot_general | solution.py:42
  373.6 9.3 %pad_maximum_fusion = f32[5120,512]{0,1:T(8,128)} fusion(f32[5120,256]{0,1:T(8,128)} %fusion.10, f32[5120,256]{0,1:T(8,128)} %bitcast.153), kind=kLoop, calls=%fused_computation.8 | loop fusion | flops 2621440 | bytes 20971520 | tf_op jit(solution)/shard_map/concatenate | solution.py:45
  382.9 11.4 %copy.62 = f32[5120,512]{1,0:T(8,128)} copy(f32[5120,512]{0,1:T(8,128)} %pad_maximum_fusion) | data formatting | bytes 20971520 | tf_op jit(solution)/shard_map/concatenate | solution.py:45
  394.3 6.2 %gather_fusion = f32[512,512]{1,0:T(8,128)S(1)} fusion(f32[5120,512]{1,0:T(8,128)} %copy.62, s32[1024]{0:T(1024)S(1)} %pad_clamp_fusion), kind=kCustom, calls=%fused_computation | custom fusion | bytes 2099200 | tf_op jit(solution)/shard_map/jit(_take)/gather | solution.py:132
  403.8 60.0 %all-reduce.6.cloned.1.call-done = f32[512,512]{1,0:T(8,128)} async-done(((f32[512,512]{1,0:T(8,128)}), f32[512,512]{1,0:T(8,128)}) %all-reduce.6.cloned.1.call-update) | async-done | bytes 1048592 | tf_op jit(solution)/shard_map/psum | solution.py:133
  463.8 39.6 %add_subtract_fusion = f32[5120,512]{1,0:T(8,128)} fusion(f32[5120,512]{1,0:T(8,128)} %reshape.194, f32[5120,512]{1,0:T(8,128)} %param.10, f32[5120,512]{1,0:T(8,128)} %reshape.190, f32[512,512]{1,0:T(8,128)} %all-reduce.6.cloned.1.call-done, f32[5120]{0:T(1024)S(1)} %fusion.47, f32[5120,256]{0,1:T(8,128)} %fusion.10, f32[5120,256]{0,1:T(8,128)} %bitcast.155), kind=kOutput, calls=%fused_computation.12 | convolution fusion | flops 16119234560 | bytes 53497856 | tf_op jit(solution)/shard_map/dot_general | solution.py:134
  (122 shorter events, 79.8 us)
Async XLA Ops:
  7.2 19.6 %copy-start.3 = (bf16[512,1024]{1,0:T(8,128)(2,1)S(1)}, bf16[512,1024]{1,0:T(8,128)(2,1)}, u32[]{:S(2)}) copy-start(bf16[512,1024]{1,0:T(8,128)(2,1)} %param.12) | copy-start | bytes 3145732
  7.2 152.2 %all-gather.2.cloned.1.call-start = ((), (), s32[]{:S(2)}) async-start(), calls=%async_computation.4 | async-start | bytes 11141120 | tf_op jit(solution)/shard_map/all_gather | solution.py:117
  7.9 46.8 %copy-start.4 = (s32[32]{0:T(128)S(1)}, s32[32]{0:T(128)}, u32[]{:S(2)}) copy-start(s32[32]{0:T(128)} %param.14) | copy-start | bytes 388
  7.9 46.8 %copy-start.5 = (s32[32]{0:T(128)S(1)}, s32[32]{0:T(128)}, u32[]{:S(2)}) copy-start(s32[32]{0:T(128)} %param.13) | copy-start | bytes 388
  19.6 31.4 %all-to-all-start = ((bf16[16,512,1,64]{1,3,2,0:T(8,128)(2,1)}), bf16[16,512,1,64]{1,3,2,0:T(8,128)(2,1)S(1)}, u32[]{:S(2)}, u32[]{:S(2)}) async-start(bf16[16,512,1,64]{1,3,2,0:T(8,128)(2,1)} %fusion.21), calls=%async_computation | async-start | bytes 2097152 | tf_op jit(solution)/shard_map/all_to_all | solution.py:76
  51.0 4.0 copy-start.1
  51.0 27.8 %all-to-all-start.2 = ((bf16[512,16,64]{0,2,1:T(8,128)(2,1)}), bf16[512,16,64]{0,2,1:T(8,128)(2,1)S(1)}, u32[]{:S(2)}, u32[]{:S(2)}) async-start(bf16[512,16,64]{0,2,1:T(8,128)(2,1)} %bitcast.29), calls=%async_computation.2 | async-start | bytes 2097152 | tf_op jit(solution)/shard_map/all_to_all | solution.py:87
  78.8 32.2 %all-to-all-start.1 = ((bf16[8,2048,64]{1,2,0:T(8,128)(2,1)}), bf16[8,2048,64]{1,2,0:T(8,128)(2,1)S(1)}, u32[]{:S(2)}, u32[]{:S(2)}) async-start(bf16[8,2048,64]{1,2,0:T(8,128)(2,1)} %copy.56), calls=%async_computation.1 | async-start | bytes 4194304 | tf_op jit(solution)/shard_map/all_to_all | solution.py:101
  111.0 35.5 %all-to-all-start.3 = ((bf16[8,2048,64]{1,2,0:T(8,128)(2,1)}), bf16[8,2048,64]{1,2,0:T(8,128)(2,1)}, u32[]{:S(2)}, u32[]{:S(2)}) async-start(bf16[8,2048,64]{1,2,0:T(8,128)(2,1)} %copy.60), calls=%async_computation.3 | async-start | bytes 4194304 | tf_op jit(solution)/shard_map/all_to_all | solution.py:102
  115.4 110.7 %all-reduce.4.cloned.1.call-start = ((), (), s32[]{:S(2)}) async-start(), calls=%async_computation.5 | async-start | bytes 2097152 | tf_op jit(solution)/shard_map/psum | solution.py:12
  161.7 302.0 %all-reduce.6.cloned.1.call-start = ((), (), s32[]{:S(2)}) async-start(), calls=%async_computation.6 | async-start | bytes 2097152 | tf_op jit(solution)/shard_map/psum | solution.py:133
  226.0 62.7 %copy-start.2 = (f32[512,512]{0,1:T(8,128)S(1)}, f32[512,512]{0,1:T(8,128)}, u32[]{:S(2)}) copy-start(f32[512,512]{0,1:T(8,128)} %all-reduce.4.cloned.1.call-done) | copy-start | bytes 3145732
  358.0 9.0 %copy-start = (f32[256,5120]{1,0:T(8,128)}, f32[256,5120]{1,0:T(8,128)S(1)}, u32[]{:S(2)}) copy-start(f32[256,5120]{1,0:T(8,128)S(1)} %fusion.4) | copy-start | bytes 15728644
Sparse Core Ops, SparseCore 0:
  10.2 101.6 all-gather.1
  161.8 64.1 all-reduce.3
  401.9 61.8 all-reduce.5
